TPU v7x, 32 devices: a whole 2x2x4 slice. The times are simulated.
32 devices in a mesh: parts: 1, dp: 32 (over z, y, x, core).
Axes of the slice: x: 2, y: 2, z: 4, core: 2. Of those that a mesh axis runs over, the one named last changes fastest.
Arguments:
- activations: bfloat16 [5120, 4, 3072], P(('parts', 'dp')), may hold values from -6 to 6
- out_grads: bfloat16 [5120, 4, 6144], P(('parts', 'dp')), may hold values from -6 to 6
- input_proj: bfloat16 [3072, 32], replicated, may hold values from -0.109375 to 0.109375
- output_proj: bfloat16 [6144, 32], replicated, may hold values from -0.078125 to 0.078125
- time_weight: float32 [8], replicated, may hold values from 0.2 to 5
- time_index: int32 [5120], P(('parts', 'dp')), may hold values from 0 to 7
- pair_ids: int32 [5120], P(('parts', 'dp')), may hold values from 0 to 5119, each once
- query_ids: int32 [128], P('parts'), may hold values from 0 to 5119
Outputs:
- scores: float32 [5120, 128], P(('parts', 'dp'))
- preconditioned: float32 [1024, 128], P('dp', 'parts')
Inputs may be any that keep to these rules, and one draw needn't show every extreme that they name: `pair_ids`: every pair id appears exactly once.
All inputs are finite; a program needn't handle non-finite values.
Results may differ from a plain program's by a relative error of at most 0.0003.
Values sent between devices are 32-bit elements; how exact they have to be, the bound alone decides.
A program may use at most 64 MiB of HBM per device.

v0:
```python
import jax
import jax.numpy as jnp
from jax import lax
from jax.sharding import PartitionSpec as P

ITERS = 4


damping = 0.5


def body(
    activations, out_grads, input_proj, output_proj, time_weight, time_index, pair_ids, query_ids
):
    highest = lax.Precision.HIGHEST
    pair_count, token_count, width_in = activations.shape
    width_out = out_grads.shape[2]
    low_rank = input_proj.shape[1]
    feature_count = low_rank * low_rank
    devices = lax.axis_size("dp")
    total_pairs = pair_count * devices
    act_low = jnp.dot(
        activations.reshape(-1, width_in), input_proj, preferred_element_type=jnp.float32
    ).reshape(pair_count, token_count, low_rank)
    grad_low = jnp.dot(
        out_grads.reshape(-1, width_out), output_proj, preferred_element_type=jnp.float32
    ).reshape(pair_count, token_count, low_rank)
    features = jnp.einsum("ptj,pti->pji", grad_low, act_low, precision=highest).reshape(
        pair_count, feature_count
    )
    step_grid = jnp.arange(time_weight.shape[0], dtype=jnp.int32)
    loss_weight = jnp.sum(
        jnp.where(time_index[:, None] == step_grid[None, :], time_weight[None, :], 0.0), axis=1
    )
    scaled_weight = loss_weight / total_pairs
    selector = (pair_ids[:, None] == query_ids[None, :]).astype(jnp.float32)
    columns = features
    query_rows = lax.psum_scatter(
        jnp.dot(columns.T, selector, precision=highest), "dp", scatter_dimension=0, tiled=True
    )
    columns = features
    fisher_rows = lax.psum_scatter(
        jnp.dot((columns * scaled_weight[:, None]).T, features, precision=highest),
        "dp",
        scatter_dimension=0,
        tiled=True,
    )

    def column_norm(residual):
        return lax.psum(jnp.sum(residual * residual, axis=0), "dp")

    solution = jnp.zeros_like(query_rows)
    residual = query_rows
    direction = query_rows
    norm_now = column_norm(residual)
    for sweep_index in range(ITERS):
        folded = jnp.dot(
            fisher_rows, lax.all_gather(direction, "dp", axis=0, tiled=True), precision=highest
        )
        image = folded + damping * direction
        step_size = norm_now / lax.psum(jnp.sum(direction * image, axis=0), "dp")
        solution = solution + step_size * direction
        residual = residual - step_size * image
        if sweep_index + 1 < ITERS:
            norm_next = column_norm(residual)
            direction = residual + norm_next / norm_now * direction
            norm_now = norm_next
    raw_scores = jnp.dot(
        features, lax.all_gather(solution, "dp", axis=0, tiled=True), precision=highest
    )
    scores = raw_scores * loss_weight[:, None] * feature_count ** (-0.5)
    return (scores, solution)


def solution(mesh):
    placed = (
        P(("parts", "dp"), None, None),
        P(("parts", "dp"), None, None),
        P(),
        P(),
        P(),
        P(("parts", "dp")),
        P(("parts", "dp")),
        P("parts"),
    )
    return jax.shard_map(
        body,
        mesh=mesh,
        in_specs=placed,
        out_specs=(P(("parts", "dp"), None), P("dp", "parts")),
        check_vma=False,
    )
```

profile of v0, /device:TPU:0, one launch (start us, length us, event | category | flops | bytes accessed | tf_op | source)
XLA Modules:
  0.0 762.3 jit_solution(15556131327835746860)
XLA Ops:
  7.2 0.0 copy-start
  7.2 0.0 reduce-scatter.3.cloned.1.call-start
  7.2 0.8 select_reduce_fusion
  8.1 0.1 copy-done
  8.2 0.0 copy-start.6
  8.2 7.8 %fusion = f32[160,4,32]{0,2,1:T(8,128)S(1)} fusion(bf16[160,4,6144]{2,1,0:T(4,128)(2,1)} %param.9, bf16[6144,32]{0,1:T(8,128)(2,1)S(1)} %copy-done), kind=kOutput, calls=%fused_computation | convolution fusion | flops 251658240 | bytes 8339456 | tf_op jit(solution)/shard_map/dot_general | solution.py:25
  16.0 0.2 copy.14
  16.2 0.0 copy-done.6
  16.2 3.5 fusion.2
  19.7 0.2 copy.15
  19.9 0.0 copy-start.4
  19.9 0.0 copy-start.5
  19.9 6.1 broadcast_multiply_fusion
  26.0 2.5 copy.16
  28.6 0.0 copy-done.4
  28.6 0.0 copy-done.5
  28.6 1.4 fusion.9
  30.0 0.0 reduce-scatter.3.cloned.1.call-update
  30.0 0.2 reduce-scatter.5.cloned.1.call-start
  30.3 2.5 copy.17
  32.8 5.1 fusion.13
  37.9 0.0 reduce-scatter.5.cloned.1.call-update
  37.9 129.0 %reduce-scatter.3.cloned.1.call-done = f32[32,128]{1,0:T(8,128)} async-done(((f32[1024,128]{1,0:T(8,128)}), f32[32,128]{1,0:T(8,128)}) %reduce-scatter.3.cloned.1.call-update) | async-done | bytes 16400 | tf_op jit(solution)/shard_map/reduce_scatter | solution.py:38
  166.9 0.0 copy-start.2
  166.9 38.8 %all_gather.15 = f32[1024,128]{1,0:T(8,128)S(1)} all-gather(f32[32,128]{1,0:T(8,128)} %reduce-scatter.3.cloned.1.call-done), channel_id=1, replica_groups=mesh['parts'=1,'dp'=32] {'dp'}, dimensions={0}, use_global_device_ids=true | all-gather | bytes 540672 | tf_op jit(solution)/shard_map/all_gather | solution.py:58
  205.7 101.3 %reduce-scatter.5.cloned.1.call-done = f32[32,1024]{1,0:T(8,128)} async-done(((f32[1024,1024]{1,0:T(8,128)}), f32[32,1024]{1,0:T(8,128)}) %reduce-scatter.5.cloned.1.call-update) | async-done | bytes 131088 | tf_op jit(solution)/shard_map/reduce_scatter | solution.py:42
  307.0 0.0 copy-start.1
  307.0 1.4 multiply_reduce_fusion.5
  308.4 36.9 %all-reduce = (f32[128]{0:T(128)S(1)}, f32[128]{0:T(128)S(1)}) all-reduce(f32[128]{0:T(128)S(1)} %get-tuple-element.3, f32[128]{0:T(128)S(1)} %get-tuple-element.2), channel_id=1, replica_groups=mesh['parts'=1,'dp'=32] {'dp'}, use_global_device_ids=true, to_apply=%region_2.3 | all-reduce | flops 256 | bytes 2048 | tf_op jit(solution)/shard_map/psum | solution.py:50
  345.3 0.7 multiply_reduce_fusion.4
  346.1 41.0 %psum.58 = f32[128]{0:T(128)S(1)} all-reduce(f32[128]{0:T(128)S(1)} %multiply_reduce_fusion.4), channel_id=1, replica_groups=mesh['parts'=1,'dp'=32] {'dp'}, use_global_device_ids=true, to_apply=%region_8.9 | all-reduce | flops 128 | bytes 1024 | tf_op jit(solution)/shard_map/psum | solution.py:50
  387.0 0.7 multiply_add_fusion.3
  387.8 42.4 %all_gather.16 = f32[1024,128]{1,0:T(8,128)S(1)} all-gather(f32[32,128]{1,0:T(8,128)S(1)} %multiply_add_fusion.3), channel_id=1, replica_groups=mesh['parts'=1,'dp'=32] {'dp'}, dimensions={0}, use_global_device_ids=true | all-gather | bytes 540672 | tf_op jit(solution)/shard_map/all_gather | solution.py:58
  430.2 1.3 multiply_reduce_fusion.3
  431.5 36.9 %psum.59 = f32[128]{0:T(128)S(1)} all-reduce(f32[128]{0:T(128)S(1)} %get-tuple-element.11), channel_id=1, replica_groups=mesh['parts'=1,'dp'=32] {'dp'}, use_global_device_ids=true, to_apply=%region_10.11 | all-reduce | flops 128 | bytes 1024 | tf_op jit(solution)/shard_map/psum | solution.py:61
  468.4 0.7 multiply_reduce_fusion.2
  469.1 41.2 %psum.60 = f32[128]{0:T(128)S(1)} all-reduce(f32[128]{0:T(128)S(1)} %get-tuple-element.6), channel_id=1, replica_groups=mesh['parts'=1,'dp'=32] {'dp'}, use_global_device_ids=true, to_apply=%region_12.13 | all-reduce | flops 128 | bytes 1024 | tf_op jit(solution)/shard_map/psum | solution.py:50
  510.4 42.1 %all_gather.17 = f32[1024,128]{1,0:T(8,128)S(1)} all-gather(f32[32,128]{1,0:T(8,128)S(1)} %multiply_add_fusion.2), channel_id=1, replica_groups=mesh['parts'=1,'dp'=32] {'dp'}, dimensions={0}, use_global_device_ids=true | all-gather | bytes 540672 | tf_op jit(solution)/shard_map/all_gather | solution.py:58
  552.5 1.3 multiply_reduce_fusion.1
  553.8 36.9 %psum.61 = f32[128]{0:T(128)S(1)} all-reduce(f32[128]{0:T(128)S(1)} %get-tuple-element.13), channel_id=1, replica_groups=mesh['parts'=1,'dp'=32] {'dp'}, use_global_device_ids=true, to_apply=%region_14.15 | all-reduce | flops 128 | bytes 1024 | tf_op jit(solution)/shard_map/psum | solution.py:61
  590.7 41.2 %psum.62 = f32[128]{0:T(128)S(1)} all-reduce(f32[128]{0:T(128)S(1)} %multiply_reduce_fusion), channel_id=1, replica_groups=mesh['parts'=1,'dp'=32] {'dp'}, use_global_device_ids=true, to_apply=%region_16.17 | all-reduce | flops 128 | bytes 1024 | tf_op jit(solution)/shard_map/psum | solution.py:50
  631.9 42.1 %all_gather.18 = f32[1024,128]{1,0:T(8,128)S(1)} all-gather(f32[32,128]{1,0:T(8,128)S(1)} %multiply_add_fusion.1), channel_id=1, replica_groups=mesh['parts'=1,'dp'=32] {'dp'}, dimensions={0}, use_global_device_ids=true | all-gather | bytes 540672 | tf_op jit(solution)/shard_map/all_gather | solution.py:58
  674.0 0.0 copy-done.1
  674.0 0.4 fusion.6
  674.4 36.9 %psum.63 = f32[128]{0:T(128)S(1)} all-reduce(f32[128]{0:T(128)S(1)} %fusion.6), channel_id=1, replica_groups=mesh['parts'=1,'dp'=32] {'dp'}, use_global_device_ids=true, to_apply=%region_18.19 | all-reduce | flops 128 | bytes 1024 | tf_op jit(solution)/shard_map/psum | solution.py:61
  711.4 0.0 copy-done.2
  711.4 0.0 copy-start.3
  711.4 41.6 %all_gather.19 = f32[1024,128]{1,0:T(8,128)S(1)} all-gather(f32[32,128]{1,0:T(8,128)S(1)} %multiply_add_fusion), channel_id=1, replica_groups=mesh['parts'=1,'dp'=32] {'dp'}, dimensions={0}, use_global_device_ids=true | all-gather | bytes 540672 | tf_op jit(solution)/shard_map/all_gather | solution.py:69
  753.0 2.5 fusion.4
  755.4 0.0 copy-done.3
  (12 shorter events, 0.1 us)
Async XLA Ops:
  7.2 1.0 copy-start
  7.2 159.7 %reduce-scatter.3.cloned.1.call-start = ((), (), s32[]{:S(2)}) async-start(), calls=%async_computation.2 | async-start | bytes 540672 | tf_op jit(solution)/shard_map/reduce_scatter | solution.py:38
  8.2 8.0 %copy-start.6 = (bf16[3072,32]{0,1:T(8,128)(2,1)S(1)}, bf16[3072,32]{0,1:T(8,128)(2,1)}, u32[]{:S(2)}) copy-start(bf16[3072,32]{0,1:T(8,128)(2,1)} %param.10) | copy-start | bytes 589828
  19.9 8.7 %copy-start.4 = (s32[160]{0:T(256)S(1)}, s32[160]{0:T(256)}, u32[]{:S(2)}) copy-start(s32[160]{0:T(256)} %param.14) | copy-start | bytes 1924
  19.9 8.7 %copy-start.5 = (s32[128]{0:T(128)S(1)}, s32[128]{0:T(128)}, u32[]{:S(2)}) copy-start(s32[128]{0:T(128)} %param.15) | copy-start | bytes 1540
  30.0 277.0 %reduce-scatter.5.cloned.1.call-start = ((), (), s32[]{:S(2)}) async-start(), calls=%async_computation.3 | async-start | bytes 4325376 | tf_op jit(solution)/shard_map/reduce_scatter | solution.py:42
  166.9 544.4 %copy-start.2 = (f32[32,128]{1,0:T(8,128)S(1)}, f32[32,128]{1,0:T(8,128)}, u32[]{:S(2)}) copy-start(f32[32,128]{1,0:T(8,128)} %reduce-scatter.3.cloned.1.call-done) | copy-start | bytes 49156
  307.0 367.0 %copy-start.1 = (f32[32,1024]{1,0:T(8,128)S(1)}, f32[32,1024]{1,0:T(8,128)}, u32[]{:S(2)}) copy-start(f32[32,1024]{1,0:T(8,128)} %reduce-scatter.5.cloned.1.call-done) | copy-start | bytes 393220
  711.4 44.1 %copy-start.3 = (f32[32,128]{1,0:T(8,128)}, f32[32,128]{1,0:T(8,128)S(1)}, u32[]{:S(2)}) copy-start(f32[32,128]{1,0:T(8,128)S(1)} %multiply_add_fusion) | copy-start | bytes 49156
Sparse Core Ops, SparseCore 0:
  30.2 136.6 reduce-scatter.2
  169.3 137.7 reduce-scatter.4
where the time goes:
time: 764 us; the launch traced here: 762 us
  blocking collectives  478 us (63%)
  waiting for transfers between devices  230 us (30%)
  matrix products  30.8 us (4%)
  between operations  14.2 us (2%)
    all_gather x4, blocking collectives, body(): lax.all_gather(direction, 'dp', axis=0, tiled=True)  165 us
    psum x4, blocking collectives, column_norm(): return lax.psum(jnp.sum(residual * residual, axis=0), 'dp')  160 us
    reduce_scatter x1, waiting for transfers between devices, body(): lax.psum_scatter(jnp.dot(columns.T, selector, precision=highest), 'dp', s...  129 us
    psum x3, blocking collectives, body(): step_size = norm_now / lax.psum(jnp.sum(direction * image, axis=0), 'dp')  111 us
    reduce_scatter x1, waiting for transfers between devices, body(): lax.psum_scatter(jnp.dot((columns * scaled_weight[:, None]).T, features,...  101 us
    all_gather x1, blocking collectives, body(): lax.all_gather(solution, 'dp', axis=0, tiled=True)  41.6 us
  transfers between devices with their start and end apart: 2, of which 2 were waited for; matrix products, arithmetic and copies ran while one was open for 1% of the time, Pallas kernels for 0%

commit v1 on v0

v1 whole, which is shorter than its diff:
```python
import functools

import jax
import jax.numpy as jnp
from jax import lax
from jax.experimental import pallas as pl
from jax.experimental.pallas import tpu as pltpu
from jax.sharding import PartitionSpec as P

ITERS = 4
DAMPING = 0.5
GROUP = 8
BANDS = GROUP // 2 + 1
F32 = jnp.float32
BF16 = jnp.bfloat16


def split(value):
    high = value.astype(BF16)
    return high, (value - high.astype(F32)).astype(BF16)


def dot_nt(a, b):
    return lax.dot_general(a, b, (((1,), (1,)), ((), ())), preferred_element_type=F32)


def flip(index, bits):
    out = index
    for bit in (1, 2, 4):
        if bits & bit:
            out = out + bit - 2 * bit * ((index // bit) % 2)
    return out


def kernel(
    count, tokens, low, pairs, msg_ref, query_ref, weight_ref, scores_ref, own_ref,
    fac, fac_t, own_t, local_t, local, feats, part, landed, fis, qpart, qlanded, qf, query,
    f_high, f_low, x_ref,
    fac_send, fac_recv, rs_send, rs_recv, qz_send, qz_recv, ag_send, ag_recv,
    fis_send, fis_recv, qf_send, qf_recv,
):
    me = lax.axis_index("dp")
    spot = me % GROUP
    base = me - spot
    level = me // GROUP
    levels = count // GROUP
    feat = low * low
    block = feat // GROUP
    piece = block // levels
    per_block = block // low
    near = (2, 4, 6)

    def send(src, dst, send_sem, recv_sem, peer):
        copy = pltpu.make_async_remote_copy(
            src_ref=src, dst_ref=dst, send_sem=send_sem, recv_sem=recv_sem,
            device_id={"dp": peer}, device_id_type=pl.DeviceIdType.MESH,
        )
        copy.start()
        return copy

    def level_peer(step):
        return ((level + step) % levels) * GROUP + spot

    class Gather:
        def __init__(self, buffer, send_sem, recv_sem, source=None):
            self.buffer, self.send_sem, self.recv_sem = buffer, send_sem, recv_sem
            src = buffer.at[spot] if source is None else source
            self.copies = {}
            for bits in near + (1,):
                self.copies[bits] = send(
                    src, buffer.at[spot], send_sem.at[bits - 1], recv_sem.at[bits - 1],
                    base + flip(spot, bits),
                )

        def relay(self):
            for bits in near:
                self.copies[bits].wait_recv()
                there = self.buffer.at[flip(spot, bits)]
                self.copies[bits + 1] = send(
                    there, there, self.send_sem.at[bits], self.recv_sem.at[bits],
                    base + flip(spot, 1),
                )

        def finish(self):
            for bits in (1, 3, 5, 7):
                self.copies[bits].wait_recv()
            for bits in range(1, GROUP):
                self.copies[bits].wait_send()

    barrier = pltpu.get_barrier_semaphore()
    peers = [base + flip(spot, bits) for bits in (1,) + near]
    peers += [level_peer(step) for step in range(1, levels)]
    for peer in peers:
        pl.semaphore_signal(
            barrier, inc=1, device_id={"dp": peer}, device_id_type=pl.DeviceIdType.MESH
        )
    pl.semaphore_wait(barrier, len(peers))

    gather = Gather(fac, fac_send, fac_recv, msg_ref)
    fac[spot] = msg_ref[...]

    own_t[...] = msg_ref[0:pairs, :].T

    def expand(read_row, act, out, start):
        total = None
        for t in range(tokens):
            term = read_row(t) * act(t)
            total = term if total is None else total + term
        out[pl.ds(start, low), :] = total

    half = tokens * low

    @pl.loop(0, low)
    def _(j):
        expand(
            lambda t: own_t[pl.ds(half + t * low + j, 1), :],
            lambda t: own_t[t * low:(t + 1) * low, :],
            local_t, pl.multiple_of(j * low, low),
        )

    local[...] = local_t[...].T

    gather.relay()
    gather.finish()

    fac_t[...] = jnp.concatenate([fac[s, 0:pairs, :] for s in range(GROUP)], axis=0).T
    extras = jnp.concatenate([fac[s, pairs:pairs + 8, 0:pairs] for s in range(GROUP)], axis=1)
    weights = extras[0:1, :]
    ids = extras[1:2, :]

    chosen = jnp.where(query_ref[...] == ids, 1.0, 0.0).astype(BF16)
    share = 2 * half // GROUP
    rows = fac_t[pl.ds(pl.multiple_of(spot * share, share), share), :]
    high, rest = rows.astype(BF16), rows
    rest = rest - high.astype(F32)
    mid, last = split(rest)
    qpart[...] = (dot_nt(last, chosen) + dot_nt(mid, chosen)) + dot_nt(high, chosen)
    q_copies = [
        send(qpart, qlanded.at[k - 1], qz_send.at[k - 1], qz_recv.at[k - 1], level_peer(k))
        for k in range(1, levels)
    ]

    for b in range(BANDS):
        first = ((spot + b) % GROUP) * per_block

        @pl.loop(0, per_block)
        def _(jj):
            expand(
                lambda t: fac_t[pl.ds(half + t * low + first + jj, 1), :],
                lambda t: fac_t[t * low:(t + 1) * low, :],
                feats, pl.multiple_of(b * block + jj * low, low),
            )

    a_high, a_low = split(feats[0:block, :] * weights)
    for b in range(BANDS):
        b_high, b_low = split(feats[b * block:(b + 1) * block, :])
        part[:, b * block:(b + 1) * block] = (
            dot_nt(a_low, b_high) + dot_nt(a_high, b_low)
        ) + dot_nt(a_high, b_high)

    def rows_of(lv):
        return pl.ds(pl.multiple_of(lv * piece, piece), piece)

    rs_copies = [
        send(
            part.at[rows_of((level + k) % levels), :], landed.at[k - 1],
            rs_send.at[k - 1], rs_recv.at[k - 1], level_peer(k),
        )
        for k in range(1, levels)
    ]
    q_total = qpart[...]
    for k in range(1, levels):
        q_copies[k - 1].wait_recv()
        q_total = q_total + qlanded[k - 1]
    qf[spot] = q_total
    q_gather = Gather(qf, qf_send, qf_recv)

    total = part[rows_of(level), :]
    for k in range(1, levels):
        rs_copies[k - 1].wait_recv()
        total = total + landed[k - 1]
    mine = fis.at[spot, rows_of(level), :]
    fis[spot, rows_of(level), :] = total
    ag_copies = [
        send(mine, mine, ag_send.at[k - 1], ag_recv.at[k - 1], level_peer(k))
        for k in range(1, levels)
    ]

    q_gather.relay()
    q_gather.finish()

    @pl.loop(0, low)
    def _(j):
        expand(
            lambda t: qf[tokens + t, pl.ds(j, 1), :],
            lambda t: qf[t],
            query, pl.multiple_of(j * low, low),
        )

    for copy in ag_copies:
        copy.wait_recv()
    f_gather = Gather(fis, fis_send, fis_recv)
    f_gather.relay()
    f_gather.finish()

    for i in range(GROUP):
        for k in range(BANDS):
            j = (i + k) % GROUP
            tile = fis[i, :, k * block:(k + 1) * block]
            high, rest = split(tile)
            f_high[i * block:(i + 1) * block, j * block:(j + 1) * block] = high
            f_low[i * block:(i + 1) * block, j * block:(j + 1) * block] = rest
            if 0 < k < BANDS - 1:
                high, rest = split(tile.T)
                f_high[j * block:(j + 1) * block, i * block:(i + 1) * block] = high
                f_low[j * block:(j + 1) * block, i * block:(i + 1) * block] = rest

    columns = query.shape[1]
    residual = query[...]
    direction = residual
    norm_now = jnp.sum(residual * residual, axis=0, keepdims=True)
    for sweep in range(ITERS):
        d_high, d_low = split(direction)
        both = jnp.dot(
            f_high[...], jnp.concatenate([d_high, d_low], axis=1), preferred_element_type=F32
        )
        image = (
            (jnp.dot(f_low[...], d_high, preferred_element_type=F32) + both[:, columns:])
            + both[:, :columns]
        ) + DAMPING * direction
        step_size = norm_now / jnp.sum(direction * image, axis=0, keepdims=True)
        if sweep == 0:
            x_ref[...] = step_size * direction
        else:
            x_ref[...] += step_size * direction
        if sweep + 1 < ITERS:
            residual = residual - step_size * image
            norm_next = jnp.sum(residual * residual, axis=0, keepdims=True)
            direction = residual + norm_next / norm_now * direction
            norm_now = norm_next

    own_rows = feat // count
    own_ref[...] = x_ref[pl.ds(pl.multiple_of(me * own_rows, own_rows), own_rows), :]
    x_high, x_low = split(x_ref[...])
    l_high, l_low = split(local[...])
    raw = (
        jnp.dot(l_low, x_high, preferred_element_type=F32)
        + jnp.dot(l_high, x_low, preferred_element_type=F32)
    ) + jnp.dot(l_high, x_high, preferred_element_type=F32)
    scores_ref[...] = raw * weight_ref[...] * feat ** (-0.5)

    for copy in q_copies + rs_copies + ag_copies:
        copy.wait_send()


def body(
    activations, out_grads, input_proj, output_proj, time_weight, time_index, pair_ids, query_ids
):
    pairs, tokens, width_in = activations.shape
    width_out = out_grads.shape[2]
    low = input_proj.shape[1]
    feat = low * low
    count = lax.axis_size("dp")
    levels = count // GROUP
    block = feat // GROUP
    piece = block // levels
    columns = query_ids.shape[0]
    width = 2 * tokens * low
    act_low = jnp.dot(
        activations.reshape(-1, width_in), input_proj, preferred_element_type=F32
    ).reshape(pairs, tokens * low)
    grad_low = jnp.dot(
        out_grads.reshape(-1, width_out), output_proj, preferred_element_type=F32
    ).reshape(pairs, tokens * low)
    grid = jnp.arange(time_weight.shape[0], dtype=jnp.int32)
    loss_weight = jnp.sum(
        jnp.where(time_index[:, None] == grid[None, :], time_weight[None, :], 0.0), axis=1
    )
    extras = jnp.stack([loss_weight / (pairs * count), pair_ids.astype(F32)])
    extras = jnp.pad(extras, ((0, 6), (0, width - pairs)))
    msg = jnp.concatenate([jnp.concatenate([act_low, grad_low], axis=1), extras], axis=0)
    group_pairs = GROUP * pairs
    dma = pltpu.SemaphoreType.DMA
    scratch = [
        pltpu.VMEM((GROUP, pairs + 8, width), F32),
        pltpu.VMEM((width, group_pairs), F32),
        pltpu.VMEM((width, pairs), F32),
        pltpu.VMEM((feat, pairs), F32),
        pltpu.VMEM((pairs, feat), F32),
        pltpu.VMEM((BANDS * block, group_pairs), F32),
        pltpu.VMEM((block, BANDS * block), F32),
        pltpu.VMEM((levels - 1, piece, BANDS * block), F32),
        pltpu.VMEM((GROUP, block, BANDS * block), F32),
        pltpu.VMEM((width // GROUP, columns), F32),
        pltpu.VMEM((levels - 1, width // GROUP, columns), F32),
        pltpu.VMEM((GROUP, width // GROUP, columns), F32),
        pltpu.VMEM((feat, columns), F32),
        pltpu.VMEM((feat, feat), BF16),
        pltpu.VMEM((feat, feat), BF16),
        pltpu.VMEM((feat, columns), F32),
        dma((GROUP - 1,)), dma((GROUP - 1,)),
        dma((levels - 1,)), dma((levels - 1,)),
        dma((levels - 1,)), dma((levels - 1,)),
        dma((levels - 1,)), dma((levels - 1,)),
        dma((GROUP - 1,)), dma((GROUP - 1,)),
        dma((GROUP - 1,)), dma((GROUP - 1,)),
    ]
    vmem = pl.BlockSpec(memory_space=pltpu.VMEM)
    scores, own = pl.pallas_call(
        functools.partial(kernel, count, tokens, low, pairs),
        out_shape=(
            jax.ShapeDtypeStruct((pairs, columns), F32),
            jax.ShapeDtypeStruct((feat // count, columns), F32),
        ),
        in_specs=[vmem] * 3,
        out_specs=(vmem, vmem),
        scratch_shapes=scratch,
        compiler_params=pltpu.CompilerParams(
            collective_id=0, has_side_effects=True, vmem_limit_bytes=48 * 1024 * 1024
        ),
    )(msg, query_ids.astype(F32)[:, None], loss_weight[:, None])
    return scores, own


def solution(mesh):
    placed = (
        P(("parts", "dp"), None, None),
        P(("parts", "dp"), None, None),
        P(),
        P(),
        P(),
        P(("parts", "dp")),
        P(("parts", "dp")),
        P("parts"),
    )
    return jax.shard_map(
        body,
        mesh=mesh,
        in_specs=placed,
        out_specs=(P(("parts", "dp"), None), P("dp", "parts")),
        check_vma=False,
    )
```

time: 764 us -> 92.2 us (0.12)
  blocking collectives: 478 us -> 0 us
  waiting for transfers between devices: 230 us -> 0 us
  Pallas kernels: 0 us -> 58.4 us
  matrix products: 30.8 us -> 8.71 us
  local copies, waits for them, and re-layouts: 5.59 us -> 21.3 us
  between operations: 14.2 us -> 0.72 us
    psum x7 -> x0, blocking collectives: 271 us -> none  [the longest x4 160 us: column_norm(): return lax.psum(jnp.sum(residual * residual, axis=0), 'dp')]
    reduce_scatter x2 -> x0, waiting for transfers between devices: 230 us -> none  [the longest x1 129 us: body(): lax.psum_scatter(jnp.dot(columns.T, selector, precision=highest), 'dp', s...]
    all_gather x5 -> x0, blocking collectives: 207 us -> none  [the longest x4 165 us: body(): lax.all_gather(direction, 'dp', axis=0, tiled=True)]
    pallas_call x0 -> x1, Pallas kernels: none -> 58.4 us  [body(): pl.pallas_call(functools.partial(kernel, count, tokens, low, pairs), out_...]
    reshape x0 -> x4, local copies, waits for them, and re-layouts: none -> 19.8 us  [the longest x1 12.5 us: body(): out_grads.reshape(-1, width_out)]
    dot_general x8 -> x0, matrix products: 19.5 us -> none  [the longest x1 6.13 us: body(): jnp.einsum('ptj,pti->pji', grad_low, act_low, precision=highest)]
  transfers between devices with their start and end apart: 2 -> 0, of which waited for: 2 -> 0; matrix products, arithmetic and copies ran while one was open for 1% -> 0% of each run, Pallas kernels for 0% -> 0%
where the time goes in v1:
time: 92.2 us; the launch traced here: 90.7 us
  Pallas kernels  58.4 us (63%)
  local copies, waits for them, and re-layouts  21.3 us (23%)
  matrix products  8.71 us (9%)
  other arithmetic  1.55 us (2%)
    pallas_call x1, Pallas kernels, body(): pl.pallas_call(functools.partial(kernel, count, tokens, low, pairs), out_...  58.4 us
    reshape x1, local copies, waits for them, and re-layouts, body(): out_grads.reshape(-1, width_out)  12.5 us
    reshape x1, local copies, waits for them, and re-layouts, body(): activations.reshape(-1, width_in)  7.12 us
    dot_general x1, matrix products, body(): jnp.dot(out_grads.reshape(-1, width_out), output_proj, preferred_element_...  5.44 us
    dot_general x1, matrix products, body(): jnp.dot(activations.reshape(-1, width_in), input_proj, preferred_element_...  3.27 us

profile of v1, /device:TPU:0, one launch (start us, length us, event | category | flops | bytes accessed | tf_op | source)
XLA Modules:
  0.0 90.7 jit_solution(1675712996246924221)
XLA Ops:
  0.6 0.0 copy-start
  0.6 0.8 select_reduce_fusion
  1.5 0.7 convert_element_type.8
  2.2 12.5 %reshape.29 = bf16[640,6144]{1,0:T(8,128)(2,1)} reshape(bf16[160,4,6144]{2,1,0:T(4,128)(2,1)} %param.9) | data formatting | bytes 15728640 | tf_op jit(solution)/shard_map/reshape | solution.py:273
  14.7 0.0 copy-done
  14.7 0.0 copy-start.1
  14.7 5.4 %fusion.1 = f32[640,32]{1,0:T(8,128)S(1)} fusion(bf16[640,6144]{1,0:T(8,128)(2,1)} %reshape.29, bf16[6144,32]{0,1:T(8,128)(2,1)S(1)} %copy-done), kind=kOutput, calls=%fused_computation.9 | convolution fusion | flops 251658240 | bytes 8339456 | tf_op jit(solution)/shard_map/dot_general | solution.py:272
  20.1 0.0 copy-start.2
  20.1 0.1 reshape.30
  20.2 7.1 %reshape.27 = bf16[640,3072]{1,0:T(8,128)(2,1)} reshape(bf16[160,4,3072]{2,1,0:T(4,128)(2,1)} %param.8) | data formatting | bytes 7864320 | tf_op jit(solution)/shard_map/reshape | solution.py:270
  27.4 0.0 copy-done.1
  27.4 3.3 %fusion = f32[640,32]{1,0:T(8,128)S(1)} fusion(bf16[640,3072]{1,0:T(8,128)(2,1)} %reshape.27, bf16[3072,32]{0,1:T(8,128)(2,1)S(1)} %copy-done.1), kind=kOutput, calls=%fused_computation.8 | convolution fusion | flops 125829120 | bytes 4210688 | tf_op jit(solution)/shard_map/dot_general | solution.py:269
  30.6 0.1 reshape.28
  30.8 0.1 copy.20.weight_ref
  30.9 0.0 copy-done.2
  30.9 0.1 copy.19.query_ref
  31.1 58.4 %shard_map.95 = (f32[160,128]{1,0:T(8,128)S(1)}, f32[32,128]{1,0:T(8,128)S(1)}) custom-call(f32[168,256]{1,0:T(8,128)S(1)} %pad_maximum_fusion.msg_ref, f32[128,1]{1,0:T(8,128)S(1)} %copy.19.query_ref, f32[160,1]{1,0:T(8,128)S(1)} %copy.20.weight_ref), custom_call_target="tpu_custom_call" | custom-call | tf_op jit(solution)/shard_map/pallas_call | solution.py:309
  89.4 0.6 copy.25
  90.1 0.6 copy.26
  (4 shorter events, 0.0 us)
Async XLA Ops:
  0.6 14.0 %copy-start = (bf16[6144,32]{0,1:T(8,128)(2,1)S(1)}, bf16[6144,32]{0,1:T(8,128)(2,1)}, u32[]{:S(2)}) copy-start(bf16[6144,32]{0,1:T(8,128)(2,1)} %param.11) | copy-start | bytes 1179652
  14.7 12.7 %copy-start.1 = (bf16[3072,32]{0,1:T(8,128)(2,1)S(1)}, bf16[3072,32]{0,1:T(8,128)(2,1)}, u32[]{:S(2)}) copy-start(bf16[3072,32]{0,1:T(8,128)(2,1)} %param.10) | copy-start | bytes 589828
  20.1 10.8 %copy-start.2 = (s32[128]{0:T(128)S(1)}, s32[128]{0:T(128)}, u32[]{:S(2)}) copy-start(s32[128]{0:T(128)} %param.15) | copy-start | bytes 1540

commit v2 on v1

--- a/solution.py
+++ b/solution.py
@@ -48,7 +48,6 @@
     block = feat // GROUP
     piece = block // levels
     per_block = block // low
-    near = (2, 4, 6)
 
     def send(src, dst, send_sem, recv_sem, peer):
         copy = pltpu.make_async_remote_copy(
@@ -62,33 +61,47 @@
         return ((level + step) % levels) * GROUP + spot
 
     class Gather:
-        def __init__(self, buffer, send_sem, recv_sem, source=None):
-            self.buffer, self.send_sem, self.recv_sem = buffer, send_sem, recv_sem
-            src = buffer.at[spot] if source is None else source
+        def __init__(self, buffer, spans, send_sem, recv_sem, source=None):
+            self.buffer, self.spans = buffer, spans
+            self.send_sem, self.recv_sem = send_sem, recv_sem
+            self.source = buffer.at[spot] if source is None else source
             self.copies = {}
-            for bits in near + (1,):
-                self.copies[bits] = send(
-                    src, buffer.at[spot], send_sem.at[bits - 1], recv_sem.at[bits - 1],
-                    base + flip(spot, bits),
-                )
-
-        def relay(self):
-            for bits in near:
-                self.copies[bits].wait_recv()
-                there = self.buffer.at[flip(spot, bits)]
-                self.copies[bits + 1] = send(
-                    there, there, self.send_sem.at[bits], self.recv_sem.at[bits],
-                    base + flip(spot, 1),
-                )
+
+        def copy(self, src, slot, bits, via, n):
+            self.copies[bits, n] = send(
+                src, self.buffer.at[slot, self.spans[n], :],
+                self.send_sem.at[bits - 1, n], self.recv_sem.at[bits - 1, n],
+                base + flip(spot, via),
+            )
+
+        def own(self, n):
+            for bits in (2, 4, 1):
+                self.copy(self.source.at[self.spans[n], :], spot, bits, bits, n)
+
+        def forward(self, bits, via, n):
+            slot = flip(spot, bits)
+            self.copy(self.buffer.at[slot, self.spans[n], :], slot, bits ^ via, via, n)
+
+        def hop(self, n):
+            for bits in (2, 4) if n % 2 == 0 else (4, 2):
+                self.copies[bits, n].wait_recv()
+                if bits == (2, 4)[n % 2]:
+                    self.forward(bits, 6 - bits, n)
+                self.forward(bits, 1, n)
+
+        def last(self, n):
+            self.copies[6, n].wait_recv()
+            self.forward(6, 1, n)
 
         def finish(self):
-            for bits in (1, 3, 5, 7):
-                self.copies[bits].wait_recv()
-            for bits in range(1, GROUP):
-                self.copies[bits].wait_send()
+            for n in range(len(self.spans)):
+                for bits in (1, 3, 5, 7):
+                    self.copies[bits, n].wait_recv()
+            for copy in self.copies.values():
+                copy.wait_send()
 
     barrier = pltpu.get_barrier_semaphore()
-    peers = [base + flip(spot, bits) for bits in (1,) + near]
+    peers = [base + flip(spot, bits) for bits in (1, 2, 4)]
     peers += [level_peer(step) for step in range(1, levels)]
     for peer in peers:
         pl.semaphore_signal(
@@ -96,10 +109,18 @@
         )
     pl.semaphore_wait(barrier, len(peers))
 
-    gather = Gather(fac, fac_send, fac_recv, msg_ref)
+    cut = (pairs // 16) * 8
+    gather = Gather(
+        fac, (pl.ds(0, cut), pl.ds(cut, pairs + 8 - cut)), fac_send, fac_recv, msg_ref
+    )
+    gather.own(0)
+    gather.own(1)
     fac[spot] = msg_ref[...]
-
-    own_t[...] = msg_ref[0:pairs, :].T
+    gather.hop(0)
+    gather.hop(1)
+    gather.last(0)
+    gather.last(1)
+    gather.finish()
 
     def expand(read_row, act, out, start):
         total = None
@@ -109,19 +130,6 @@
         out[pl.ds(start, low), :] = total
 
     half = tokens * low
-
-    @pl.loop(0, low)
-    def _(j):
-        expand(
-            lambda t: own_t[pl.ds(half + t * low + j, 1), :],
-            lambda t: own_t[t * low:(t + 1) * low, :],
-            local_t, pl.multiple_of(j * low, low),
-        )
-
-    local[...] = local_t[...].T
-
-    gather.relay()
-    gather.finish()
 
     fac_t[...] = jnp.concatenate([fac[s, 0:pairs, :] for s in range(GROUP)], axis=0).T
     extras = jnp.concatenate([fac[s, pairs:pairs + 8, 0:pairs] for s in range(GROUP)], axis=1)
@@ -168,12 +176,25 @@
         )
         for k in range(1, levels)
     ]
+    own_t[...] = msg_ref[0:pairs, :].T
+
+    @pl.loop(0, low)
+    def _(j):
+        expand(
+            lambda t: own_t[pl.ds(half + t * low + j, 1), :],
+            lambda t: own_t[t * low:(t + 1) * low, :],
+            local_t, pl.multiple_of(j * low, low),
+        )
+
+    local[...] = local_t[...].T
+
     q_total = qpart[...]
     for k in range(1, levels):
         q_copies[k - 1].wait_recv()
         q_total = q_total + qlanded[k - 1]
     qf[spot] = q_total
-    q_gather = Gather(qf, qf_send, qf_recv)
+    q_gather = Gather(qf, (pl.ds(0, share),), qf_send, qf_recv)
+    q_gather.own(0)
 
     total = part[rows_of(level), :]
     for k in range(1, levels):
@@ -186,7 +207,22 @@
         for k in range(1, levels)
     ]
 
-    q_gather.relay()
+    f_gather = Gather(
+        fis, [rows_of((level + n) % levels) for n in range(levels)], fis_send, fis_recv
+    )
+    f_gather.own(0)
+    q_gather.hop(0)
+    for n in range(1, levels):
+        ag_copies[levels - n - 1].wait_recv()
+        f_gather.own(n)
+        f_gather.hop(n - 1)
+        if n >= 2:
+            f_gather.last(n - 2)
+    f_gather.hop(levels - 1)
+    if levels > 1:
+        f_gather.last(levels - 2)
+    f_gather.last(levels - 1)
+    q_gather.last(0)
     q_gather.finish()
 
     @pl.loop(0, low)
@@ -197,10 +233,6 @@
             query, pl.multiple_of(j * low, low),
         )
 
-    for copy in ag_copies:
-        copy.wait_recv()
-    f_gather = Gather(fis, fis_send, fis_recv)
-    f_gather.relay()
     f_gather.finish()
 
     for i in range(GROUP):
@@ -266,12 +298,15 @@
     piece = block // levels
     columns = query_ids.shape[0]
     width = 2 * tokens * low
-    act_low = jnp.dot(
-        activations.reshape(-1, width_in), input_proj, preferred_element_type=F32
-    ).reshape(pairs, tokens * low)
-    grad_low = jnp.dot(
-        out_grads.reshape(-1, width_out), output_proj, preferred_element_type=F32
-    ).reshape(pairs, tokens * low)
+    act_low = jnp.einsum(
+        "ptk,ki->pti", activations, input_proj, preferred_element_type=F32
+    )
+    grad_low = jnp.einsum(
+        "ptk,ki->pti", out_grads, output_proj, preferred_element_type=F32
+    )
+    act_low, grad_low = lax.optimization_barrier((act_low, grad_low))
+    act_low = act_low.reshape(pairs, tokens * low)
+    grad_low = grad_low.reshape(pairs, tokens * low)
     grid = jnp.arange(time_weight.shape[0], dtype=jnp.int32)
     loss_weight = jnp.sum(
         jnp.where(time_index[:, None] == grid[None, :], time_weight[None, :], 0.0), axis=1
@@ -298,12 +333,12 @@
         pltpu.VMEM((feat, feat), BF16),
         pltpu.VMEM((feat, feat), BF16),
         pltpu.VMEM((feat, columns), F32),
-        dma((GROUP - 1,)), dma((GROUP - 1,)),
+        dma((GROUP - 1, 2)), dma((GROUP - 1, 2)),
         dma((levels - 1,)), dma((levels - 1,)),
         dma((levels - 1,)), dma((levels - 1,)),
         dma((levels - 1,)), dma((levels - 1,)),
-        dma((GROUP - 1,)), dma((GROUP - 1,)),
-        dma((GROUP - 1,)), dma((GROUP - 1,)),
+        dma((GROUP - 1, levels)), dma((GROUP - 1, levels)),
+        dma((GROUP - 1, 1)), dma((GROUP - 1, 1)),
     ]
     vmem = pl.BlockSpec(memory_space=pltpu.VMEM)
     scores, own = pl.pallas_call(

time: 92.2 us -> 68.9 us (0.75); the launches traced: 90.7 us -> 68.7 us
  local copies, waits for them, and re-layouts: 21.3 us -> 2.63 us
  Pallas kernels: 58.4 us -> 55.6 us
  other arithmetic: 1.55 us -> 0.12 us
    reshape x4 -> x2, local copies, waits for them, and re-layouts: 19.8 us -> 0.19 us  [the longest x1 0.1 us: body(): act_low = act_low.reshape(pairs, tokens * low)]
    pallas_call x1, Pallas kernels: 58.4 us -> 55.6 us  [body(): pl.pallas_call(functools.partial(kernel, count, tokens, low, pairs), out_...]
    unnamed x8 -> x16, local copies, waits for them, and re-layouts: 1.26 us -> 2.22 us
where the time goes in v2:
time: 68.9 us; the launch traced here: 68.7 us
  Pallas kernels  55.6 us (81%)
  matrix products  9.58 us (14%)
  local copies, waits for them, and re-layouts  2.63 us (4%)
  between operations  0.79 us (1%)
    pallas_call x1, Pallas kernels, body(): pl.pallas_call(functools.partial(kernel, count, tokens, low, pairs), out_...  55.6 us
    dot_general x1, matrix products, body(): jnp.einsum('ptk,ki->pti', out_grads, output_proj, preferred_element_type=...  8.22 us
    unnamed x16, local copies, waits for them, and re-layouts  2.22 us

profile of v2, /device:TPU:0, one launch (start us, length us, event | category | flops | bytes accessed | tf_op | source)
XLA Modules:
  0.0 68.7 jit_solution(16130349576600994497)
XLA Ops:
  0.6 0.0 copy-start
  0.6 0.0 copy-start.5
  0.7 0.0 copy-start.4
  0.7 0.0 copy-start.3
  0.7 0.0 copy-start.1
  0.7 0.0 copy-start.2
  0.7 0.9 %copy-done = bf16[6144,32]{0,1:T(8,128)(2,1)S(1)} copy-done((bf16[6144,32]{0,1:T(8,128)(2,1)S(1)}, bf16[6144,32]{0,1:T(8,128)(2,1)}, u32[]{:S(2)}) %copy-start) | copy-done | bytes 393240
  1.6 0.0 copy-start.6
  1.6 8.2 %fusion = f32[160,4,32]{0,2,1:T(8,128)S(1)} fusion(bf16[160,4,6144]{2,1,0:T(4,128)(2,1)} %param.9, bf16[6144,32]{0,1:T(8,128)(2,1)S(1)} %copy-done), kind=kOutput, calls=%fused_computation | convolution fusion | flops 251658240 | bytes 8339456 | tf_op jit(solution)/shard_map/ptk,ki->pti/dot_general | solution.py:304
  9.9 0.0 copy-done.5
  9.9 0.0 copy-done.4
  9.9 1.4 %fusion.2 = f32[160,4,32]{0,2,1:T(8,128)S(1)} fusion(bf16[160,4,3072]{2,1,0:T(4,128)(2,1)S(1)} %copy-done.4, bf16[3072,32]{0,1:T(8,128)(2,1)S(1)} %copy-done.5), kind=kOutput, calls=%fused_computation.2 | convolution fusion | flops 125829120 | bytes 4210688 | tf_op jit(solution)/shard_map/ptk,ki->pti/dot_general | solution.py:301
  11.2 0.1 copy.23
  11.3 0.1 copy.24
  11.4 0.0 copy-done.3
  11.5 0.0 copy-done.1
  11.5 0.1 select_reduce_fusion
  11.6 0.0 copy-done.2
  11.6 0.1 copy.26.weight_ref
  11.7 0.0 copy-done.6
  11.8 0.1 copy.25.query_ref
  11.9 55.6 %shard_map.95 = (f32[160,128]{1,0:T(8,128)S(1)}, f32[32,128]{1,0:T(8,128)S(1)}) custom-call(f32[168,256]{1,0:T(8,128)S(1)} %pad_maximum_fusion.msg_ref, f32[128,1]{1,0:T(8,128)S(1)} %copy.25.query_ref, f32[160,1]{1,0:T(8,128)S(1)} %copy.26.weight_ref), custom_call_target="tpu_custom_call" | custom-call | tf_op jit(solution)/shard_map/pallas_call | solution.py:344
  67.4 0.6 copy.33
  68.1 0.6 copy.34
  (5 shorter events, 0.0 us)
Async XLA Ops:
  0.6 1.0 %copy-start = (bf16[6144,32]{0,1:T(8,128)(2,1)S(1)}, bf16[6144,32]{0,1:T(8,128)(2,1)}, u32[]{:S(2)}) copy-start(bf16[6144,32]{0,1:T(8,128)(2,1)} %param.11) | copy-start | bytes 1179652
  0.6 9.2 %copy-start.5 = (bf16[3072,32]{0,1:T(8,128)(2,1)S(1)}, bf16[3072,32]{0,1:T(8,128)(2,1)}, u32[]{:S(2)}) copy-start(bf16[3072,32]{0,1:T(8,128)(2,1)} %param.10) | copy-start | bytes 589828
  0.7 9.2 %copy-start.4 = (bf16[160,4,3072]{2,1,0:T(4,128)(2,1)S(1)}, bf16[160,4,3072]{2,1,0:T(4,128)(2,1)}, u32[]{:S(2)}) copy-start(bf16[160,4,3072]{2,1,0:T(4,128)(2,1)} %param.8) | copy-start | bytes 11796484
  0.7 10.8 %copy-start.3 = (f32[8]{0:T(128)S(1)}, f32[8]{0:T(128)}, u32[]{:S(2)}) copy-start(f32[8]{0:T(128)} %param.12) | copy-start | bytes 100
  0.7 10.8 %copy-start.1 = (s32[160]{0:T(256)S(1)}, s32[160]{0:T(256)}, u32[]{:S(2)}) copy-start(s32[160]{0:T(256)} %param.13) | copy-start | bytes 1924
  0.7 10.9 %copy-start.2 = (s32[160]{0:T(256)S(1)}, s32[160]{0:T(256)}, u32[]{:S(2)}) copy-start(s32[160]{0:T(256)} %param.14) | copy-start | bytes 1924
  1.6 10.1 %copy-start.6 = (s32[128]{0:T(128)S(1)}, s32[128]{0:T(128)}, u32[]{:S(2)}) copy-start(s32[128]{0:T(128)} %param.15) | copy-start | bytes 1540

commit v3 on v2

--- a/solution.py
+++ b/solution.py
@@ -148,8 +148,13 @@
         for k in range(1, levels)
     ]
 
+    def rows_of(lv):
+        return pl.ds(pl.multiple_of(lv * piece, piece), piece)
+
+    rs_copies = []
     for b in range(BANDS):
         first = ((spot + b) % GROUP) * per_block
+        band = pl.ds(b * block, block)
 
         @pl.loop(0, per_block)
         def _(jj):
@@ -159,23 +164,20 @@
                 feats, pl.multiple_of(b * block + jj * low, low),
             )
 
-    a_high, a_low = split(feats[0:block, :] * weights)
-    for b in range(BANDS):
+        if b == 0:
+            a_high, a_low = split(feats[0:block, :] * weights)
         b_high, b_low = split(feats[b * block:(b + 1) * block, :])
         part[:, b * block:(b + 1) * block] = (
             dot_nt(a_low, b_high) + dot_nt(a_high, b_low)
         ) + dot_nt(a_high, b_high)
-
-    def rows_of(lv):
-        return pl.ds(pl.multiple_of(lv * piece, piece), piece)
-
-    rs_copies = [
-        send(
-            part.at[rows_of((level + k) % levels), :], landed.at[k - 1],
-            rs_send.at[k - 1], rs_recv.at[k - 1], level_peer(k),
-        )
-        for k in range(1, levels)
-    ]
+        rs_copies += [
+            send(
+                part.at[rows_of((level + k) % levels), band], landed.at[k - 1, :, band],
+                rs_send.at[b, k - 1], rs_recv.at[b, k - 1], level_peer(k),
+            )
+            for k in range(1, levels)
+        ]
+
     own_t[...] = msg_ref[0:pairs, :].T
 
     @pl.loop(0, low)
@@ -196,9 +198,10 @@
     q_gather = Gather(qf, (pl.ds(0, share),), qf_send, qf_recv)
     q_gather.own(0)
 
+    for copy in rs_copies:
+        copy.wait_recv()
     total = part[rows_of(level), :]
     for k in range(1, levels):
-        rs_copies[k - 1].wait_recv()
         total = total + landed[k - 1]
     mine = fis.at[spot, rows_of(level), :]
     fis[spot, rows_of(level), :] = total
@@ -334,7 +337,7 @@
         pltpu.VMEM((feat, feat), BF16),
         pltpu.VMEM((feat, columns), F32),
         dma((GROUP - 1, 2)), dma((GROUP - 1, 2)),
-        dma((levels - 1,)), dma((levels - 1,)),
+        dma((BANDS, levels - 1)), dma((BANDS, levels - 1)),
         dma((levels - 1,)), dma((levels - 1,)),
         dma((levels - 1,)), dma((levels - 1,)),
         dma((GROUP - 1, levels)), dma((GROUP - 1, levels)),

time: 68.9 us -> 69.3 us (level)
  the two profiles are of different devices: /device:TPU:0 before, /device:TPU:11 now
where the time goes in v3:
time: 69.3 us; the launch traced here: 69.2 us
  Pallas kernels  56.1 us (81%)
  matrix products  9.58 us (14%)
  local copies, waits for them, and re-layouts  2.63 us (4%)
  between operations  0.79 us (1%)
    pallas_call x1, Pallas kernels, body(): pl.pallas_call(functools.partial(kernel, count, tokens, low, pairs), out_...  56.1 us
    dot_general x1, matrix products, body(): jnp.einsum('ptk,ki->pti', out_grads, output_proj, preferred_element_type=...  8.22 us
    unnamed x16, local copies, waits for them, and re-layouts  2.22 us

profile of v3, /device:TPU:11, one launch (start us, length us, event | category | flops | bytes accessed | tf_op | source)
XLA Modules:
  0.0 69.2 jit_solution(7872241202501437496)
XLA Ops:
  0.6 0.0 copy-start
  0.6 0.0 copy-start.5
  0.7 0.0 copy-start.4
  0.7 0.0 copy-start.3
  0.7 0.0 copy-start.1
  0.7 0.0 copy-start.2
  0.7 0.9 %copy-done = bf16[6144,32]{0,1:T(8,128)(2,1)S(1)} copy-done((bf16[6144,32]{0,1:T(8,128)(2,1)S(1)}, bf16[6144,32]{0,1:T(8,128)(2,1)}, u32[]{:S(2)}) %copy-start) | copy-done | bytes 393240
  1.6 0.0 copy-start.6
  1.6 8.2 %fusion = f32[160,4,32]{0,2,1:T(8,128)S(1)} fusion(bf16[160,4,6144]{2,1,0:T(4,128)(2,1)} %param.9, bf16[6144,32]{0,1:T(8,128)(2,1)S(1)} %copy-done), kind=kOutput, calls=%fused_computation | convolution fusion | flops 251658240 | bytes 8339456 | tf_op jit(solution)/shard_map/ptk,ki->pti/dot_general | solution.py:307
  9.9 0.0 copy-done.5
  9.9 0.0 copy-done.4
  9.9 1.4 %fusion.2 = f32[160,4,32]{0,2,1:T(8,128)S(1)} fusion(bf16[160,4,3072]{2,1,0:T(4,128)(2,1)S(1)} %copy-done.4, bf16[3072,32]{0,1:T(8,128)(2,1)S(1)} %copy-done.5), kind=kOutput, calls=%fused_computation.2 | convolution fusion | flops 125829120 | bytes 4210688 | tf_op jit(solution)/shard_map/ptk,ki->pti/dot_general | solution.py:304
  11.2 0.1 copy.23
  11.3 0.1 copy.24
  11.4 0.0 copy-done.3
  11.5 0.0 copy-done.1
  11.5 0.1 select_reduce_fusion
  11.6 0.0 copy-done.2
  11.6 0.1 copy.26.weight_ref
  11.7 0.0 copy-done.6
  11.8 0.1 copy.25.query_ref
  11.9 56.1 %shard_map.95 = (f32[160,128]{1,0:T(8,128)S(1)}, f32[32,128]{1,0:T(8,128)S(1)}) custom-call(f32[168,256]{1,0:T(8,128)S(1)} %pad_maximum_fusion.msg_ref, f32[128,1]{1,0:T(8,128)S(1)} %copy.25.query_ref, f32[160,1]{1,0:T(8,128)S(1)} %copy.26.weight_ref), custom_call_target="tpu_custom_call" | custom-call | tf_op jit(solution)/shard_map/pallas_call | solution.py:347
  67.9 0.6 copy.33
  68.6 0.6 copy.34
  (5 shorter events, 0.0 us)
Async XLA Ops:
  0.6 1.0 %copy-start = (bf16[6144,32]{0,1:T(8,128)(2,1)S(1)}, bf16[6144,32]{0,1:T(8,128)(2,1)}, u32[]{:S(2)}) copy-start(bf16[6144,32]{0,1:T(8,128)(2,1)} %param.11) | copy-start | bytes 1179652
  0.6 9.2 %copy-start.5 = (bf16[3072,32]{0,1:T(8,128)(2,1)S(1)}, bf16[3072,32]{0,1:T(8,128)(2,1)}, u32[]{:S(2)}) copy-start(bf16[3072,32]{0,1:T(8,128)(2,1)} %param.10) | copy-start | bytes 589828
  0.7 9.2 %copy-start.4 = (bf16[160,4,3072]{2,1,0:T(4,128)(2,1)S(1)}, bf16[160,4,3072]{2,1,0:T(4,128)(2,1)}, u32[]{:S(2)}) copy-start(bf16[160,4,3072]{2,1,0:T(4,128)(2,1)} %param.8) | copy-start | bytes 11796484
  0.7 10.8 %copy-start.3 = (f32[8]{0:T(128)S(1)}, f32[8]{0:T(128)}, u32[]{:S(2)}) copy-start(f32[8]{0:T(128)} %param.12) | copy-start | bytes 100
  0.7 10.8 %copy-start.1 = (s32[160]{0:T(256)S(1)}, s32[160]{0:T(256)}, u32[]{:S(2)}) copy-start(s32[160]{0:T(256)} %param.13) | copy-start | bytes 1924
  0.7 10.9 %copy-start.2 = (s32[160]{0:T(256)S(1)}, s32[160]{0:T(256)}, u32[]{:S(2)}) copy-start(s32[160]{0:T(256)} %param.14) | copy-start | bytes 1924
  1.6 10.1 %copy-start.6 = (s32[128]{0:T(128)S(1)}, s32[128]{0:T(128)}, u32[]{:S(2)}) copy-start(s32[128]{0:T(128)} %param.15) | copy-start | bytes 1540
